TPU v7x, 128 devices: a whole 4x4x4 slice. The times are simulated.
128 devices in a mesh: segment: 4 (over x), seq: 32 (over z, y, core).
Axes of the slice: x: 4, y: 4, z: 4, core: 2. Of those that a mesh axis runs over, the one named last changes fastest.
Arguments:
- token_ids: int32 [256], P('seq'), may hold values from 0 to 511
- cached_len: int32 [2], replicated, may hold values from 128 to 786432
- embed: bfloat16 [512, 8192], P(None, 'seq'), may hold values from -6 to 6
- gain: float32 [4, 8192], P('segment'), may hold values from 0.1 to 1.9
- w_in: bfloat16 [4, 8192, 3, 8192], P('segment', None, None, 'seq'), may hold values from -0.0625 to 0.0625
- short_filter: float32 [4, 7, 3, 8192], P('segment', None, None, 'seq'), may hold values from -2.5 to 2.5
- long_filter: float32 [4, 128, 512], P('segment', None, 'seq'), may hold values from -0.5 to 0.5
- w_out: bfloat16 [4, 8192, 8192], P('segment', None, 'seq'), may hold values from -0.0625 to 0.0625
- short_cycle: bfloat16 [4, 2, 128, 3, 8192], P('segment', None, None, None, 'seq'), may hold values from -6 to 6
- long_cycle: bfloat16 [4, 2, 128, 8192], P('segment', None, None, 'seq'), may hold values from -6 to 6
Outputs:
- section_out: bfloat16 [4, 256, 8192], P('segment', None, 'seq')
- new_short_cycle: bfloat16 [4, 2, 128, 3, 8192], P('segment', None, None, None, 'seq')
- new_long_cycle: bfloat16 [4, 2, 128, 8192], P('segment', None, None, 'seq')
All inputs are finite; a program needn't handle non-finite values.
Results may differ from a plain program's by a relative error of at most 0.023.
Values may be sent and summed in bfloat16 or wider, within the bound.
A program may use at most 128 MiB of HBM per device.

v0:
```python
import jax
import jax.numpy as jnp
from jax import lax
from jax.sharding import PartitionSpec as P

D = 8192
G = 512
VOCAB = 512
SHORT = 7
LONG = 128
REQUESTS = 2


def from_behind(block, axis, distance):
    devices = range(lax.axis_size(axis))
    route = [(i - distance, i) for i in devices if i - distance in devices]
    return lax.ppermute(block, axis, route)


def cycle_rows(cycle, offset):
    doubled = jnp.concatenate([cycle, cycle], axis=0)
    return lax.dynamic_slice_in_dim(doubled, offset, cycle.shape[0], 0)


def local(
    token_ids,
    cached_len,
    embed,
    gain,
    w_in,
    short_filter,
    long_filter,
    w_out,
    short_cycle,
    long_cycle,
):
    my_segment = lax.axis_index("segment")
    segments = lax.axis_size("segment")
    ids_all = lax.all_gather(token_ids, "seq", axis=0, tiled=True)
    tokens = ids_all.shape[0]
    appended = tokens // REQUESTS
    channels = embed.shape[1]
    vocab_ids = jnp.arange(VOCAB, dtype=jnp.int32)
    one_hot = (ids_all[:, None] == vocab_ids[None, :]).astype(jnp.bfloat16)
    start_rows = jnp.dot(one_hot, embed, preferred_element_type=jnp.float32).astype(jnp.bfloat16)
    gain_row = gain[0]
    proj_in = w_in[0].reshape(D, 3 * channels)
    short_taps = short_filter[0]
    kernel = jnp.repeat(long_filter[0], D // G, axis=1)[::-1][:, None, :]
    proj_out = w_out[0]
    short_cache = short_cycle[0]
    long_cache = long_cycle[0]
    every_request = list(range(REQUESTS))
    current = start_rows
    result_rows = jnp.zeros_like(start_rows)
    short_result = short_cache
    long_result = long_cache
    for turn_number in range(segments):
        number = len(every_request)
        gathered = lax.all_gather(current, "seq", axis=1, tiled=True)
        widened = gathered.astype(jnp.float32)
        scaling = lax.rsqrt(jnp.mean(widened * widened, axis=1, keepdims=True) + 1e-06)
        normed = (widened * scaling * gain_row[None, :]).astype(jnp.bfloat16)
        projected = jnp.dot(normed, proj_in, preferred_element_type=jnp.float32)
        projected = projected.astype(jnp.bfloat16).reshape(number * appended, 3, channels)
        mixed_parts = []
        short_cycles = []
        long_cycles = []
        for position, request in enumerate(every_request):
            prefix = lax.dynamic_index_in_dim(cached_len, request, 0, keepdims=False)
            own_rows = projected[position * appended : (position + 1) * appended]
            short_old = lax.dynamic_index_in_dim(short_cache, request, 0, keepdims=False)
            long_old = lax.dynamic_index_in_dim(long_cache, request, 0, keepdims=False)
            extended = jnp.concatenate([cycle_rows(short_old, prefix % LONG), own_rows], axis=0)
            wide_ext = extended.astype(jnp.float32)
            filtered = jnp.zeros((appended, 3, channels), jnp.float32)
            for tap_index in range(SHORT):
                filtered = (
                    filtered
                    + short_taps[tap_index][None]
                    * wide_ext[LONG - tap_index : LONG - tap_index + appended]
                )
            product = (filtered[:, 1] * filtered[:, 2]).astype(jnp.bfloat16)
            carried = jnp.concatenate([cycle_rows(long_old, prefix % LONG), product], axis=0)
            convolved = lax.conv_general_dilated(
                carried[1:].astype(jnp.float32)[None],
                kernel,
                window_strides=(1,),
                padding="VALID",
                dimension_numbers=("NWC", "WIO", "NWC"),
                feature_group_count=channels,
                precision=lax.Precision.HIGHEST,
            )[0]
            mixed_parts.append((filtered[:, 0] * convolved).astype(jnp.bfloat16))
            backward = (LONG - (prefix + appended) % LONG) % LONG
            short_cycles.append(cycle_rows(extended[appended:], backward))
            long_cycles.append(cycle_rows(carried[appended:], backward))
        mixed = jnp.concatenate(mixed_parts, axis=0)
        initial = jnp.zeros((number * appended, channels), jnp.float32)
        shard_piece = lax.all_gather(mixed, "seq", axis=1, tiled=True)
        weight_rows = lax.slice_in_dim(proj_out, 0, shard_piece.shape[1], axis=0)
        summed = initial + jnp.dot(shard_piece, weight_rows, preferred_element_type=jnp.float32)
        output_rows = (current.astype(jnp.float32) + summed).astype(jnp.bfloat16)
        output_rows, short_cycles, long_cycles = (output_rows, short_cycles, long_cycles)
        is_mine = my_segment == turn_number
        result_rows = jnp.where(is_mine, output_rows, result_rows)
        short_result = jnp.where(is_mine, jnp.stack(short_cycles), short_result)
        long_result = jnp.where(is_mine, jnp.stack(long_cycles), long_result)
        if turn_number + 1 < segments:
            received = from_behind(output_rows, "segment", 1)
            current = jnp.where(my_segment == 0, start_rows, received)
    return (result_rows[None], short_result[None], long_result[None])


def solution(mesh):
    in_specs = (
        P("seq"),
        P(),
        P(None, "seq"),
        P("segment", None),
        P("segment", None, None, "seq"),
        P("segment", None, None, "seq"),
        P("segment", None, "seq"),
        P("segment", None, "seq"),
        P("segment", None, None, None, "seq"),
        P("segment", None, None, "seq"),
    )
    out_specs = (
        P("segment", None, "seq"),
        P("segment", None, None, None, "seq"),
        P("segment", None, None, "seq"),
    )
    return jax.shard_map(local, mesh=mesh, in_specs=in_specs, out_specs=out_specs, check_vma=False)
```

profile of v0, /device:TPU:1, one launch (start us, length us, event | category | flops | bytes accessed | tf_op | source)
XLA Modules:
  0.0 538.5 jit_solution(9733577705821494347)
XLA Ops:
  10.0 15.7 %all-reduce = s32[256]{0:T(256)S(1)} all-reduce(s32[256]{0:T(256)S(1)} %dynamic-update-slice), channel_id=1, replica_groups=mesh['segment'=4,'seq'=32] {'seq'}, use_global_device_ids=true, to_apply=%add | all-reduce | flops 256 | bytes 2048
  32.1 16.7 %copy.58 = bf16[1,8192,3,256]{1,3,2,0:T(8,128)(2,1)} copy(bf16[1,8192,3,256]{3,1,2,0:T(8,128)(2,1)} %param.14) | data formatting | bytes 25165824 | tf_op args[4]
  50.2 26.2 %all-gather.9.cloned.1.call-done = bf16[256,8192]{1,0:T(8,128)(2,1)} async-done(((bf16[256,256]{1,0:T(8,128)(2,1)}), bf16[256,8192]{1,0:T(8,128)(2,1)}) %all-gather.9.cloned.1.call-update) | async-done | bytes 4194320 | tf_op jit(solution)/shard_map/all_gather | solution.py:60
  76.3 3.3 fusion
  79.8 8.2 %fusion.36 = bf16[256,768]{1,0:T(8,128)(2,1)S(1)} fusion(bf16[8192,768]{0,1:T(8,128)(2,1)} %bitcast.197, bf16[256,8192]{1,0:T(8,128)(2,1)S(1)} %copy-done.2, f32[8192]{0:T(1024)S(1)} %bitcast.236, f32[256]{0:T(256)S(1)} %add_rsqrt_fusion.3), kind=kOutput, calls=%fused_computation.40 | convolution fusion | flops 3229810688 | bytes 17204224 | tf_op jit(solution)/shard_map/dot_general | solution.py:64
  93.3 48.9 %all-gather.11.cloned.1.call-done = bf16[256,8192]{1,0:T(8,128)(2,1)} async-done(((bf16[256,256]{1,0:T(8,128)(2,1)}), bf16[256,8192]{1,0:T(8,128)(2,1)}) %all-gather.11.cloned.1.call-update) | async-done | bytes 4194320 | tf_op jit(solution)/shard_map/all_gather | solution.py:100
  142.2 4.7 fusion.51
  146.9 3.1 collective-permute-start
  153.7 50.4 %all-gather.13.cloned.1.call-done = bf16[256,8192]{1,0:T(8,128)(2,1)} async-done(((bf16[256,256]{1,0:T(8,128)(2,1)}), bf16[256,8192]{1,0:T(8,128)(2,1)}) %all-gather.13.cloned.1.call-update) | async-done | bytes 4194320 | tf_op jit(solution)/shard_map/all_gather | solution.py:60
  204.2 3.3 fusion.3
  207.6 8.2 %fusion.39 = bf16[256,768]{1,0:T(8,128)(2,1)S(1)} fusion(bf16[8192,768]{0,1:T(8,128)(2,1)} %bitcast.198, bf16[256,8192]{1,0:T(8,128)(2,1)S(1)} %copy-done.4, f32[256]{0:T(256)S(1)} %add_rsqrt_fusion.2, f32[8192]{0:T(1024)S(1)} %bitcast.237), kind=kOutput, calls=%fused_computation.41 | convolution fusion | flops 3229810688 | bytes 17204224 | tf_op jit(solution)/shard_map/dot_general | solution.py:64
  221.1 48.9 %all-gather.15.cloned.1.call-done = bf16[256,8192]{1,0:T(8,128)(2,1)} async-done(((bf16[256,256]{1,0:T(8,128)(2,1)}), bf16[256,8192]{1,0:T(8,128)(2,1)}) %all-gather.15.cloned.1.call-update) | async-done | bytes 4194320 | tf_op jit(solution)/shard_map/all_gather | solution.py:100
  270.0 4.7 add_convert_fusion.2
  274.8 3.1 collective-permute-start.1
  281.8 50.2 %all-gather.17.cloned.1.call-done = bf16[256,8192]{1,0:T(8,128)(2,1)} async-done(((bf16[256,256]{1,0:T(8,128)(2,1)}), bf16[256,8192]{1,0:T(8,128)(2,1)}) %all-gather.17.cloned.1.call-update) | async-done | bytes 4194320 | tf_op jit(solution)/shard_map/all_gather | solution.py:60
  332.0 3.3 fusion.6
  335.4 8.2 %fusion.42 = bf16[256,768]{1,0:T(8,128)(2,1)S(1)} fusion(bf16[8192,768]{0,1:T(8,128)(2,1)} %bitcast.199, bf16[256,8192]{1,0:T(8,128)(2,1)S(1)} %copy-done.5, f32[256]{0:T(256)S(1)} %add_rsqrt_fusion.1, f32[8192]{0:T(1024)S(1)} %bitcast.238), kind=kOutput, calls=%fused_computation.42 | convolution fusion | flops 3229810688 | bytes 17204224 | tf_op jit(solution)/shard_map/dot_general | solution.py:64
  349.0 48.9 %all-gather.19.cloned.1.call-done = bf16[256,8192]{1,0:T(8,128)(2,1)} async-done(((bf16[256,256]{1,0:T(8,128)(2,1)}), bf16[256,8192]{1,0:T(8,128)(2,1)}) %all-gather.19.cloned.1.call-update) | async-done | bytes 4194320 | tf_op jit(solution)/shard_map/all_gather | solution.py:100
  397.9 4.7 add_convert_fusion.1
  409.3 50.6 %all-gather.21.cloned.1.call-done = bf16[256,8192]{1,0:T(8,128)(2,1)} async-done(((bf16[256,256]{1,0:T(8,128)(2,1)}), bf16[256,8192]{1,0:T(8,128)(2,1)}) %all-gather.21.cloned.1.call-update) | async-done | bytes 4194320 | tf_op jit(solution)/shard_map/all_gather | solution.py:60
  459.9 3.3 fusion.9
  463.3 8.2 %fusion.45 = bf16[256,768]{1,0:T(8,128)(2,1)S(1)} fusion(bf16[8192,768]{0,1:T(8,128)(2,1)} %bitcast.200, bf16[256,8192]{1,0:T(8,128)(2,1)S(1)} %copy-done.3, f32[256]{0:T(256)S(1)} %add_rsqrt_fusion, f32[8192]{0:T(1024)S(1)} %bitcast.239), kind=kOutput, calls=%fused_computation.43 | convolution fusion | flops 3229810688 | bytes 17204224 | tf_op jit(solution)/shard_map/dot_general | solution.py:64
  484.2 41.8 %all-gather.23.cloned.1.call-done = bf16[256,8192]{1,0:T(8,128)(2,1)} async-done(((bf16[256,256]{1,0:T(8,128)(2,1)}), bf16[256,8192]{1,0:T(8,128)(2,1)}) %all-gather.23.cloned.1.call-update) | async-done | bytes 4194320 | tf_op jit(solution)/shard_map/all_gather | solution.py:100
  526.0 5.4 %fusion.146 = bf16[1,256,256]{2,1,0:T(8,128)(2,1)} fusion(bf16[256,256]{1,0:T(8,128)(2,1)S(1)} %copy-done.8, bf16[256,256]{1,0:T(8,128)(2,1)} %copy-done.23, bf16[256,256]{1,0:T(8,128)(2,1)S(1)} %copy-done.22, bf16[256,256]{1,0:T(8,128)(2,1)S(1)} %copy-done.20, pred[]{:T(512)S(6)} %eq.67, pred[]{:T(512)S(6)} %eq.66, pred[]{:T(512)S(6)} %eq.62, ...), kind=kOutput, calls=%fused_computation.241 | convolution fusion | flops 1074200576 | bytes 9043972 | tf_op jit(solution)/shard_map/dot_general | solution.py:102
  (192 shorter events, 47.1 us)
Async XLA Ops:
  7.2 18.6 %copy-start = (bf16[512,256]{1,0:T(8,128)(2,1)S(1)}, bf16[512,256]{1,0:T(8,128)(2,1)}, u32[]{:S(2)}) copy-start(bf16[512,256]{1,0:T(8,128)(2,1)} %param.12) | copy-start | bytes 786436
  7.2 69.2 %all-gather.9.cloned.1.call-start = ((), (), s32[]{:S(2)}) async-start(), calls=%async_computation | async-start | bytes 4325376 | tf_op jit(solution)/shard_map/all_gather | solution.py:60
  26.7 115.5 %all-gather.11.cloned.1.call-start = ((), (), s32[]{:S(2)}) async-start(), calls=%async_computation.1 | async-start | bytes 4325376 | tf_op jit(solution)/shard_map/all_gather | solution.py:100
  32.1 17.5 %copy-start.7 = (bf16[1,2,128,3,256]{4,2,3,1,0:T(8,128)(2,1)S(1)}, bf16[1,2,128,3,256]{4,2,3,1,0:T(8,128)(2,1)}, u32[]{:S(2)}) copy-start(bf16[1,2,128,3,256]{4,2,3,1,0:T(8,128)(2,1)} %param.18) | copy-start | bytes 1179652
  48.9 30.7 %copy-start.24 = (f32[1,8192]{1,0:T(1,128)S(1)}, f32[1,8192]{1,0:T(1,128)}, u32[]{:S(2)}) copy-start(f32[1,8192]{1,0:T(1,128)} %param.13) | copy-start | bytes 98308
  49.2 295.3 %copy-start.13 = (f32[128,1,256]{2,1,0:T(1,128)}, f32[128,1,256]{2,1,0:T(1,128)S(1)}, u32[]{:S(2)}) copy-start(f32[128,1,256]{2,1,0:T(1,128)S(1)} %copy.62) | copy-start | bytes 393220
  91.1 51.1 %copy-start.6 = (bf16[256,256]{1,0:T(8,128)(2,1)S(1)}, bf16[256,256]{1,0:T(8,128)(2,1)}, u32[]{:S(2)}) copy-start(bf16[256,256]{1,0:T(8,128)(2,1)} %convolution_convert_fusion) | copy-start | bytes 393220
  93.2 110.9 %all-gather.13.cloned.1.call-start = ((), (), s32[]{:S(2)}) async-start(), calls=%async_computation.2 | async-start | bytes 4325376 | tf_op jit(solution)/shard_map/all_gather | solution.py:60
  146.9 68.9 %copy-start.19 = (bf16[256,256]{1,0:T(8,128)(2,1)}, bf16[256,256]{1,0:T(8,128)(2,1)S(1)}, u32[]{:S(2)}) copy-start(bf16[256,256]{1,0:T(8,128)(2,1)S(1)} %fusion.51) | copy-start | bytes 393220
  146.9 5.7 %collective-permute-start = (bf16[256,256]{1,0:T(8,128)(2,1)S(1)}, bf16[256,256]{1,0:T(8,128)(2,1)S(1)}, u32[]{:S(2)}, u32[]{:S(2)}) collective-permute-start(bf16[256,256]{1,0:T(8,128)(2,1)S(1)} %fusion.51), channel_id=1, source_target_pairs={{0,32},{32,64},{64,96},{1,33},{33,65},{65,97},{2,34},{34,66},{66,9... | collective-permute-start | bytes 393224 | tf_op jit(solution)/shard_map/ppermute | solution.py:17
  153.4 116.7 %all-gather.15.cloned.1.call-start = ((), (), s32[]{:S(2)}) async-start(), calls=%async_computation.3 | async-start | bytes 4325376 | tf_op jit(solution)/shard_map/all_gather | solution.py:100
  218.9 51.1 %copy-start.9 = (bf16[256,256]{1,0:T(8,128)(2,1)S(1)}, bf16[256,256]{1,0:T(8,128)(2,1)}, u32[]{:S(2)}) copy-start(bf16[256,256]{1,0:T(8,128)(2,1)} %broadcast_select_fusion.2) | copy-start | bytes 393220
  221.1 110.9 %all-gather.17.cloned.1.call-start = ((), (), s32[]{:S(2)}) async-start(), calls=%async_computation.4 | async-start | bytes 4325376 | tf_op jit(solution)/shard_map/all_gather | solution.py:60
  274.8 68.9 %copy-start.21 = (bf16[256,256]{1,0:T(8,128)(2,1)}, bf16[256,256]{1,0:T(8,128)(2,1)S(1)}, u32[]{:S(2)}) copy-start(bf16[256,256]{1,0:T(8,128)(2,1)S(1)} %add_convert_fusion.2) | copy-start | bytes 393220
  274.8 5.7 %collective-permute-start.1 = (bf16[256,256]{1,0:T(8,128)(2,1)S(1)}, bf16[256,256]{1,0:T(8,128)(2,1)S(1)}, u32[]{:S(2)}, u32[]{:S(2)}) collective-permute-start(bf16[256,256]{1,0:T(8,128)(2,1)S(1)} %add_convert_fusion.2), channel_id=1, source_target_pairs={{0,32},{32,64},{64,96},{1,33},{33,65},{65,97},{2,34},{34,66},{66,9... | collective-permute-start | bytes 393224 | tf_op jit(solution)/shard_map/ppermute | solution.py:17
  281.2 116.7 %all-gather.19.cloned.1.call-start = ((), (), s32[]{:S(2)}) async-start(), calls=%async_computation.5 | async-start | bytes 4325376 | tf_op jit(solution)/shard_map/all_gather | solution.py:100
  346.9 51.1 %copy-start.10 = (bf16[256,256]{1,0:T(8,128)(2,1)S(1)}, bf16[256,256]{1,0:T(8,128)(2,1)}, u32[]{:S(2)}) copy-start(bf16[256,256]{1,0:T(8,128)(2,1)} %broadcast_select_fusion.1) | copy-start | bytes 393220
  349.0 110.9 %all-gather.21.cloned.1.call-start = ((), (), s32[]{:S(2)}) async-start(), calls=%async_computation.6 | async-start | bytes 4325376 | tf_op jit(solution)/shard_map/all_gather | solution.py:60
  402.7 60.5 %copy-start.23 = (bf16[256,256]{1,0:T(8,128)(2,1)}, bf16[256,256]{1,0:T(8,128)(2,1)S(1)}, u32[]{:S(2)}) copy-start(bf16[256,256]{1,0:T(8,128)(2,1)S(1)} %add_convert_fusion.1) | copy-start | bytes 393220
  402.7 5.7 %collective-permute-start.2 = (bf16[256,256]{1,0:T(8,128)(2,1)S(1)}, bf16[256,256]{1,0:T(8,128)(2,1)S(1)}, u32[]{:S(2)}, u32[]{:S(2)}) collective-permute-start(bf16[256,256]{1,0:T(8,128)(2,1)S(1)} %add_convert_fusion.1), channel_id=1, source_target_pairs={{0,32},{32,64},{64,96},{1,33},{33,65},{65,97},{2,34},{34,66},{66,9... | collective-permute-start | bytes 393224 | tf_op jit(solution)/shard_map/ppermute | solution.py:17
  409.1 116.9 %all-gather.23.cloned.1.call-start = ((), (), s32[]{:S(2)}) async-start(), calls=%async_computation.7 | async-start | bytes 4325376 | tf_op jit(solution)/shard_map/all_gather | solution.py:100
  479.7 46.3 %copy-start.8 = (bf16[256,256]{1,0:T(8,128)(2,1)S(1)}, bf16[256,256]{1,0:T(8,128)(2,1)}, u32[]{:S(2)}) copy-start(bf16[256,256]{1,0:T(8,128)(2,1)} %broadcast_select_fusion) | copy-start | bytes 393220
  479.7 46.3 %copy-start.20 = (bf16[256,256]{1,0:T(8,128)(2,1)S(1)}, bf16[256,256]{1,0:T(8,128)(2,1)}, u32[]{:S(2)}) copy-start(bf16[256,256]{1,0:T(8,128)(2,1)} %copy-done.19) | copy-start | bytes 393220
  479.7 46.3 %copy-start.22 = (bf16[256,256]{1,0:T(8,128)(2,1)S(1)}, bf16[256,256]{1,0:T(8,128)(2,1)}, u32[]{:S(2)}) copy-start(bf16[256,256]{1,0:T(8,128)(2,1)} %copy-done.21) | copy-start | bytes 393220
  (12 other events, 80.1 us)
Sparse Core Ops, SparseCore 0:
  26.8 49.4 all-gather.8
  93.4 48.7 all-gather.10
  153.5 50.6 all-gather.12
  221.2 48.7 all-gather.14
  281.3 50.6 all-gather.16
  349.1 48.7 all-gather.18
  409.2 50.6 all-gather.20
  477.2 48.7 all-gather.22
where the time goes:
time: 547 us; the launch traced here: 538 us
  waiting for transfers between devices  374 us (68%)
  matrix products  64.9 us (12%)
  other arithmetic  26.7 us (5%)
  local copies, waits for them, and re-layouts  25.4 us (5%)
  between operations  21.3 us (4%)
  blocking collectives  15.7 us (3%)
  starting transfers between devices  10.6 us (2%)
    all_gather x4, waiting for transfers between devices, local(): shard_piece = lax.all_gather(mixed, 'seq', axis=1, tiled=True)  189 us
    all_gather x4, waiting for transfers between devices, local(): gathered = lax.all_gather(current, 'seq', axis=1, tiled=True)  177 us
    dot_general x4, matrix products, local(): projected = jnp.dot(normed, proj_in, preferred_element_type=jnp.float32)  33 us
    unnamed x58, local copies, waits for them, and re-layouts  19.8 us
    dot_general x4, matrix products, local(): jnp.dot(shard_piece, weight_rows, preferred_element_type=jnp.float32)  19.5 us
    unnamed x1, blocking collectives  15.7 us
    reduce_sum x4, other arithmetic, local(): jnp.mean(widened * widened, axis=1, keepdims=True) + 1e-06  13 us
    conv_general_dilated x8, matrix products, local(): lax.conv_general_dilated(carried[1:].astype(jnp.float32)[None], kernel, w...  11.5 us
  transfers between devices with their start and end apart: 11, of which 11 were waited for; matrix products, arithmetic and copies ran while one was open for 5% of the time, Pallas kernels for 0%

commit v1 on v0

--- a/solution.py
+++ b/solution.py
@@ -97,7 +97,9 @@
             long_cycles.append(cycle_rows(carried[appended:], backward))
         mixed = jnp.concatenate(mixed_parts, axis=0)
         initial = jnp.zeros((number * appended, channels), jnp.float32)
-        shard_piece = lax.all_gather(mixed, "seq", axis=1, tiled=True)
+        shard_piece = jnp.concatenate(
+            lax.all_to_all(jnp.stack([mixed] * lax.axis_size("seq")), "seq", 0, 0), axis=1
+        )
         weight_rows = lax.slice_in_dim(proj_out, 0, shard_piece.shape[1], axis=0)
         summed = initial + jnp.dot(shard_piece, weight_rows, preferred_element_type=jnp.float32)
         output_rows = (current.astype(jnp.float32) + summed).astype(jnp.bfloat16)

time: 547 us -> 566 us (1.035)
  the two profiles are of different devices: /device:TPU:1 before, /device:TPU:0 now
where the time goes in v1:
time: 566 us; the launch traced here: 557 us
  waiting for transfers between devices  222 us (39%)
  blocking collectives  188 us (33%)
  matrix products  54.5 us (10%)
  local copies, waits for them, and re-layouts  29.7 us (5%)
  other arithmetic  24 us (4%)
  between operations  21.2 us (4%)
  starting transfers between devices  17 us (3%)
    all_to_all x3, blocking collectives, local(): lax.all_to_all(jnp.stack([mixed] * lax.axis_size('seq')), 'seq', 0, 0)  170 us
    all_gather x4, waiting for transfers between devices, local(): gathered = lax.all_gather(current, 'seq', axis=1, tiled=True)  167 us
    all_to_all x1, waiting for transfers between devices, local(): lax.all_to_all(jnp.stack([mixed] * lax.axis_size('seq')), 'seq', 0, 0)  46.2 us
    dot_general x4, matrix products, local(): projected = jnp.dot(normed, proj_in, preferred_element_type=jnp.float32)  33 us
    unnamed x64, local copies, waits for them, and re-layouts  19.9 us
    unnamed x1, blocking collectives  18.3 us
    reduce_sum x4, other arithmetic, local(): jnp.mean(widened * widened, axis=1, keepdims=True) + 1e-06  13 us
  transfers between devices with their start and end apart: 8, of which 8 were waited for; matrix products, arithmetic and copies ran while one was open for 4% of the time, Pallas kernels for 0%

profile of v1, /device:TPU:0, one launch (start us, length us, event | category | flops | bytes accessed | tf_op | source)
XLA Modules:
  0.0 556.6 jit_solution(495866418033696045)
XLA Ops:
  10.0 18.3 %all-reduce = s32[256]{0:T(256)S(1)} all-reduce(s32[256]{0:T(256)S(1)} %dynamic-update-slice), channel_id=1, replica_groups=mesh['segment'=4,'seq'=32] {'seq'}, use_global_device_ids=true, to_apply=%add | all-reduce | flops 256 | bytes 2048
  34.7 16.8 %copy.62 = bf16[1,8192,3,256]{1,3,2,0:T(8,128)(2,1)} copy(bf16[1,8192,3,256]{3,1,2,0:T(8,128)(2,1)} %param.14) | data formatting | bytes 25165824 | tf_op args[4]
  52.8 22.3 %all-gather.5.cloned.1.call-done = bf16[256,8192]{1,0:T(8,128)(2,1)} async-done(((bf16[256,256]{1,0:T(8,128)(2,1)}), bf16[256,8192]{1,0:T(8,128)(2,1)}) %all-gather.5.cloned.1.call-update) | async-done | bytes 4194320 | tf_op jit(solution)/shard_map/all_gather | solution.py:60
  75.2 3.3 fusion
  78.6 8.2 %fusion.36 = bf16[256,768]{1,0:T(8,128)(2,1)S(1)} fusion(bf16[8192,768]{0,1:T(8,128)(2,1)} %bitcast.212, bf16[256,8192]{1,0:T(8,128)(2,1)S(1)} %copy-done.5, f32[8192]{0:T(1024)S(1)} %bitcast.251, f32[256]{0:T(256)S(1)} %add_rsqrt_fusion.3), kind=kOutput, calls=%fused_computation.40 | convolution fusion | flops 3229810688 | bytes 17204224 | tf_op jit(solution)/shard_map/dot_general | solution.py:64
  92.0 56.5 %all_to_all.20 = bf16[32,256,256]{1,2,0:T(8,128)(2,1)S(1)} all-to-all(bf16[32,256,256]{1,2,0:T(8,128)(2,1)S(1)} %stack.56), channel_id=1, replica_groups=mesh['segment'=4,'seq'=32] {'seq'}, dimensions={0} | all-to-all | bytes 8388608 | tf_op jit(solution)/shard_map/all_to_all | solution.py:101
  149.8 3.9 collective-permute-start
  157.5 48.4 %all-gather.7.cloned.1.call-done = bf16[256,8192]{1,0:T(8,128)(2,1)} async-done(((bf16[256,256]{1,0:T(8,128)(2,1)}), bf16[256,8192]{1,0:T(8,128)(2,1)}) %all-gather.7.cloned.1.call-update) | async-done | bytes 4194320 | tf_op jit(solution)/shard_map/all_gather | solution.py:60
  205.9 3.3 fusion.3
  209.3 8.2 %fusion.39 = bf16[256,768]{1,0:T(8,128)(2,1)S(1)} fusion(bf16[8192,768]{0,1:T(8,128)(2,1)} %bitcast.213, bf16[256,8192]{1,0:T(8,128)(2,1)S(1)} %copy-done.6, f32[256]{0:T(256)S(1)} %add_rsqrt_fusion.2, f32[8192]{0:T(1024)S(1)} %bitcast.252), kind=kOutput, calls=%fused_computation.41 | convolution fusion | flops 3229810688 | bytes 17204224 | tf_op jit(solution)/shard_map/dot_general | solution.py:64
  222.7 56.5 %all_to_all.21 = bf16[32,256,256]{1,2,0:T(8,128)(2,1)S(1)} all-to-all(bf16[32,256,256]{1,2,0:T(8,128)(2,1)S(1)} %stack.57), channel_id=1, replica_groups=mesh['segment'=4,'seq'=32] {'seq'}, dimensions={0} | all-to-all | bytes 8388608 | tf_op jit(solution)/shard_map/all_to_all | solution.py:101
  280.5 3.4 collective-permute-start.1
  283.9 3.0 collective-permute-done.1
  287.8 48.2 %all-gather.9.cloned.1.call-done = bf16[256,8192]{1,0:T(8,128)(2,1)} async-done(((bf16[256,256]{1,0:T(8,128)(2,1)}), bf16[256,8192]{1,0:T(8,128)(2,1)}) %all-gather.9.cloned.1.call-update) | async-done | bytes 4194320 | tf_op jit(solution)/shard_map/all_gather | solution.py:60
  336.0 3.3 fusion.6
  339.5 8.2 %fusion.42 = bf16[256,768]{1,0:T(8,128)(2,1)S(1)} fusion(bf16[8192,768]{0,1:T(8,128)(2,1)} %bitcast.214, bf16[256,8192]{1,0:T(8,128)(2,1)S(1)} %copy-done.7, f32[256]{0:T(256)S(1)} %add_rsqrt_fusion.1, f32[8192]{0:T(1024)S(1)} %bitcast.253), kind=kOutput, calls=%fused_computation.42 | convolution fusion | flops 3229810688 | bytes 17204224 | tf_op jit(solution)/shard_map/dot_general | solution.py:64
  352.9 56.5 %all_to_all.22 = bf16[32,256,256]{1,2,0:T(8,128)(2,1)S(1)} all-to-all(bf16[32,256,256]{1,2,0:T(8,128)(2,1)S(1)} %stack.58), channel_id=1, replica_groups=mesh['segment'=4,'seq'=32] {'seq'}, dimensions={0} | all-to-all | bytes 8388608 | tf_op jit(solution)/shard_map/all_to_all | solution.py:101
  410.8 3.6 collective-permute-start.2
  417.8 48.4 %all-gather.11.cloned.1.call-done = bf16[256,8192]{1,0:T(8,128)(2,1)} async-done(((bf16[256,256]{1,0:T(8,128)(2,1)}), bf16[256,8192]{1,0:T(8,128)(2,1)}) %all-gather.11.cloned.1.call-update) | async-done | bytes 4194320 | tf_op jit(solution)/shard_map/all_gather | solution.py:60
  466.3 3.3 fusion.9
  469.7 8.2 %fusion.45 = bf16[256,768]{1,0:T(8,128)(2,1)S(1)} fusion(bf16[8192,768]{0,1:T(8,128)(2,1)} %bitcast.215, bf16[256,8192]{1,0:T(8,128)(2,1)S(1)} %copy-done.8, f32[256]{0:T(256)S(1)} %add_rsqrt_fusion, f32[8192]{0:T(1024)S(1)} %bitcast.254), kind=kOutput, calls=%fused_computation.43 | convolution fusion | flops 3229810688 | bytes 17204224 | tf_op jit(solution)/shard_map/dot_general | solution.py:64
  485.1 5.8 %all-to-all-start.3 = ((bf16[32,256,256]{1,2,0:T(8,128)(2,1)}), bf16[32,256,256]{1,2,0:T(8,128)(2,1)}, u32[]{:S(2)}, u32[]{:S(2)}) async-start(bf16[32,256,256]{1,2,0:T(8,128)(2,1)} %stack.59), calls=%async_computation.3 | async-start | bytes 8388608 | tf_op jit(solution)/shard_map/all_to_all | solution.py:101
  498.1 46.2 %all-to-all-done.3 = bf16[32,256,256]{1,2,0:T(8,128)(2,1)} async-done(((bf16[32,256,256]{1,2,0:T(8,128)(2,1)}), bf16[32,256,256]{1,2,0:T(8,128)(2,1)}, u32[]{:S(2)}, u32[]{:S(2)}) %all-to-all-start.3) | async-done | bytes 4194336 | tf_op jit(solution)/shard_map/all_to_all | solution.py:101
  544.4 5.5 fusion.146
  (199 shorter events, 46.2 us)
Async XLA Ops:
  7.2 21.1 %copy-start = (bf16[512,256]{1,0:T(8,128)(2,1)S(1)}, bf16[512,256]{1,0:T(8,128)(2,1)}, u32[]{:S(2)}) copy-start(bf16[512,256]{1,0:T(8,128)(2,1)} %param.12) | copy-start | bytes 786436
  7.2 68.0 %all-gather.5.cloned.1.call-start = ((), (), s32[]{:S(2)}) async-start(), calls=%async_computation.4 | async-start | bytes 4325376 | tf_op jit(solution)/shard_map/all_gather | solution.py:60
  29.3 176.6 %all-gather.7.cloned.1.call-start = ((), (), s32[]{:S(2)}) async-start(), calls=%async_computation.5 | async-start | bytes 4325376 | tf_op jit(solution)/shard_map/all_gather | solution.py:60
  51.5 26.9 %copy-start.27 = (f32[1,8192]{1,0:T(1,128)S(1)}, f32[1,8192]{1,0:T(1,128)}, u32[]{:S(2)}) copy-start(f32[1,8192]{1,0:T(1,128)} %param.13) | copy-start | bytes 98308
  51.9 296.7 %copy-start.22 = (f32[128,1,256]{2,1,0:T(1,128)}, f32[128,1,256]{2,1,0:T(1,128)S(1)}, u32[]{:S(2)}) copy-start(f32[128,1,256]{2,1,0:T(1,128)S(1)} %copy.66) | copy-start | bytes 393220
  92.0 56.5 %copy-start.2 = (bf16[1,8192,256]{2,1,0:T(8,128)(2,1)S(1)}, bf16[1,8192,256]{2,1,0:T(8,128)(2,1)}, u32[]{:S(2)}) copy-start(bf16[1,8192,256]{2,1,0:T(8,128)(2,1)} %param.17) | copy-start | bytes 12582916
  92.0 56.5 %copy-start.9 = (bf16[256,256]{1,0:T(8,128)(2,1)S(1)}, bf16[256,256]{1,0:T(8,128)(2,1)}, u32[]{:S(2)}) copy-start(bf16[256,256]{1,0:T(8,128)(2,1)} %convolution_convert_fusion) | copy-start | bytes 393220
  149.8 67.7 %copy-start.14 = (bf16[256,256]{1,0:T(8,128)(2,1)}, bf16[256,256]{1,0:T(8,128)(2,1)S(1)}, u32[]{:S(2)}) copy-start(bf16[256,256]{1,0:T(8,128)(2,1)S(1)} %fusion.51) | copy-start | bytes 393220
  149.8 6.9 %collective-permute-start = (bf16[256,256]{1,0:T(8,128)(2,1)S(1)}, bf16[256,256]{1,0:T(8,128)(2,1)S(1)}, u32[]{:S(2)}, u32[]{:S(2)}) collective-permute-start(bf16[256,256]{1,0:T(8,128)(2,1)S(1)} %fusion.51), channel_id=1, source_target_pairs={{0,32},{32,64},{64,96},{1,33},{33,65},{65,97},{2,34},{34,66},{66,9... | collective-permute-start | bytes 393224 | tf_op jit(solution)/shard_map/ppermute | solution.py:17
  157.4 178.6 %all-gather.9.cloned.1.call-start = ((), (), s32[]{:S(2)}) async-start(), calls=%async_computation.6 | async-start | bytes 4325376 | tf_op jit(solution)/shard_map/all_gather | solution.py:60
  222.7 56.5 %copy-start.3 = (bf16[1,8192,256]{2,1,0:T(8,128)(2,1)S(1)}, bf16[1,8192,256]{2,1,0:T(8,128)(2,1)}, u32[]{:S(2)}) copy-start(bf16[1,8192,256]{2,1,0:T(8,128)(2,1)} %param.17) | copy-start | bytes 12582916
  222.7 56.5 %copy-start.12 = (bf16[256,256]{1,0:T(8,128)(2,1)S(1)}, bf16[256,256]{1,0:T(8,128)(2,1)}, u32[]{:S(2)}) copy-start(bf16[256,256]{1,0:T(8,128)(2,1)} %broadcast_select_fusion.2) | copy-start | bytes 393220
  280.5 67.2 %copy-start.16 = (bf16[256,256]{1,0:T(8,128)(2,1)}, bf16[256,256]{1,0:T(8,128)(2,1)S(1)}, u32[]{:S(2)}) copy-start(bf16[256,256]{1,0:T(8,128)(2,1)S(1)} %add_convert_fusion.2) | copy-start | bytes 393220
  280.5 6.4 %collective-permute-start.1 = (bf16[256,256]{1,0:T(8,128)(2,1)S(1)}, bf16[256,256]{1,0:T(8,128)(2,1)S(1)}, u32[]{:S(2)}, u32[]{:S(2)}) collective-permute-start(bf16[256,256]{1,0:T(8,128)(2,1)S(1)} %add_convert_fusion.2), channel_id=1, source_target_pairs={{0,32},{32,64},{64,96},{1,33},{33,65},{65,97},{2,34},{34,66},{66,9... | collective-permute-start | bytes 393224 | tf_op jit(solution)/shard_map/ppermute | solution.py:17
  287.6 178.7 %all-gather.11.cloned.1.call-start = ((), (), s32[]{:S(2)}) async-start(), calls=%async_computation.7 | async-start | bytes 4325376 | tf_op jit(solution)/shard_map/all_gather | solution.py:60
  352.9 56.5 %copy-start.4 = (bf16[1,8192,256]{2,1,0:T(8,128)(2,1)S(1)}, bf16[1,8192,256]{2,1,0:T(8,128)(2,1)}, u32[]{:S(2)}) copy-start(bf16[1,8192,256]{2,1,0:T(8,128)(2,1)} %param.17) | copy-start | bytes 12582916
  352.9 56.5 %copy-start.13 = (bf16[256,256]{1,0:T(8,128)(2,1)S(1)}, bf16[256,256]{1,0:T(8,128)(2,1)}, u32[]{:S(2)}) copy-start(bf16[256,256]{1,0:T(8,128)(2,1)} %broadcast_select_fusion.1) | copy-start | bytes 393220
  410.7 58.8 %copy-start.18 = (bf16[256,256]{1,0:T(8,128)(2,1)}, bf16[256,256]{1,0:T(8,128)(2,1)S(1)}, u32[]{:S(2)}) copy-start(bf16[256,256]{1,0:T(8,128)(2,1)S(1)} %add_convert_fusion.1) | copy-start | bytes 393220
  410.8 6.4 %collective-permute-start.2 = (bf16[256,256]{1,0:T(8,128)(2,1)S(1)}, bf16[256,256]{1,0:T(8,128)(2,1)S(1)}, u32[]{:S(2)}, u32[]{:S(2)}) collective-permute-start(bf16[256,256]{1,0:T(8,128)(2,1)S(1)} %add_convert_fusion.1), channel_id=1, source_target_pairs={{0,32},{32,64},{64,96},{1,33},{33,65},{65,97},{2,34},{34,66},{66,9... | collective-permute-start | bytes 393224 | tf_op jit(solution)/shard_map/ppermute | solution.py:17
  485.1 59.2 %all-to-all-start.3 = ((bf16[32,256,256]{1,2,0:T(8,128)(2,1)}), bf16[32,256,256]{1,2,0:T(8,128)(2,1)}, u32[]{:S(2)}, u32[]{:S(2)}) async-start(bf16[32,256,256]{1,2,0:T(8,128)(2,1)} %stack.59), calls=%async_computation.3 | async-start | bytes 8388608 | tf_op jit(solution)/shard_map/all_to_all | solution.py:101
  493.6 50.8 %copy-start.11 = (bf16[256,256]{1,0:T(8,128)(2,1)S(1)}, bf16[256,256]{1,0:T(8,128)(2,1)}, u32[]{:S(2)}) copy-start(bf16[256,256]{1,0:T(8,128)(2,1)} %broadcast_select_fusion) | copy-start | bytes 393220
  493.6 50.7 %copy-start.15 = (bf16[256,256]{1,0:T(8,128)(2,1)S(1)}, bf16[256,256]{1,0:T(8,128)(2,1)}, u32[]{:S(2)}) copy-start(bf16[256,256]{1,0:T(8,128)(2,1)} %copy-done.14) | copy-start | bytes 393220
  493.6 50.7 %copy-start.17 = (bf16[256,256]{1,0:T(8,128)(2,1)S(1)}, bf16[256,256]{1,0:T(8,128)(2,1)}, u32[]{:S(2)}) copy-start(bf16[256,256]{1,0:T(8,128)(2,1)} %copy-done.16) | copy-start | bytes 393220
  493.6 50.7 %copy-start.19 = (bf16[256,256]{1,0:T(8,128)(2,1)S(1)}, bf16[256,256]{1,0:T(8,128)(2,1)}, u32[]{:S(2)}) copy-start(bf16[256,256]{1,0:T(8,128)(2,1)} %copy-done.18) | copy-start | bytes 393220
  (12 other events, 95.4 us)
Sparse Core Ops, SparseCore 0:
  29.4 45.7 all-gather.4
  157.6 48.2 all-gather.6
  287.7 48.2 all-gather.8
  418.0 48.2 all-gather.10
